TPU v7x, 256 devices: a whole 4x4x8 slice. The times are simulated.
256 devices in a mesh: rows: 4 (over x), chan: 8 (over y, z_lo), filt: 8 (over z_hi, core).
Axes of the slice: x: 4, y: 4, z: 8 (z_hi: 4, z_lo: 2; z = z_hi * 2 + z_lo), core: 2. Of those that a mesh axis runs over, the one named last changes fastest.
Arguments:
- images: bfloat16 [16, 2048, 2048], P('rows', 'chan', 'filt'), may hold values from -6 to 6
- first_weight: bfloat16 [2048, 1024], P('chan', 'filt'), may hold values from -0.125 to 0.125
- group_weight: bfloat16 [3, 3, 32, 1024], P(None, None, None, 'filt'), may hold values from -0.375 to 0.375
- third_weight: bfloat16 [1024, 2048], P('chan', 'filt'), may hold values from -0.1875 to 0.1875
- out_grad: bfloat16 [16, 2048, 2048], P('rows', 'chan', 'filt'), may hold values from -6 to 6
Outputs:
- block_out: bfloat16 [16, 2048, 2048], P('rows', 'chan', 'filt')
- images_grad: float32 [16, 2048, 2048], P('rows', 'chan', 'filt')
- first_grad: float32 [2048, 1024], P('chan', 'filt')
- group_grad: float32 [3, 3, 32, 1024], P(None, None, None, 'filt')
- third_grad: float32 [1024, 2048], P('chan', 'filt')
All inputs are finite; a program needn't handle non-finite values.
Results may differ from a plain program's by a relative error of at most 0.006.
Values may be sent and summed in bfloat16 or wider, within the bound.
No kernel may reach another device: no remote copies, remote signals or barrier semaphores. Data moves between devices by JAX's collectives and lax.ppermute only.
A program may use at most 128 MiB of HBM per device.

v0:
```python
import jax
import jax.numpy as jnp
from jax import lax
from jax.sharding import PartitionSpec as P


def extended(block, sides, width):
    for axis, dim in sides:
        count = lax.axis_size(axis)
        forward = [(i, i + 1) for i in range(count - 1)]
        backward = [(target, source) for source, target in forward]
        low = lax.ppermute(
            lax.slice_in_dim(block, block.shape[dim] - width, None, axis=dim), axis, forward
        )
        high = lax.ppermute(lax.slice_in_dim(block, 0, width, axis=dim), axis, backward)
        block = jnp.concatenate([low, block, high], axis=dim)
    return block


def silu_slope(values):
    logistic = jax.nn.sigmoid(values)
    return logistic * (1.0 + values * (1.0 - logistic))


def group_conv(padded, kernel, groups_here):
    result = lax.conv_general_dilated(
        padded[None],
        kernel,
        (1, 1),
        "VALID",
        dimension_numbers=("NHWC", "HWIO", "NHWC"),
        feature_group_count=groups_here,
        preferred_element_type=jnp.float32,
    )
    return result[0]


def transposed_kernel(kernel, group_size, groups_here):
    pieces = kernel.reshape(3, 3, group_size, groups_here, group_size)
    swapped = jnp.transpose(pieces, (0, 1, 4, 3, 2)).reshape(
        3, 3, group_size, groups_here * group_size
    )
    return swapped[::-1, ::-1]


def kernel_partial(padded_first, group_delta, group_size, groups_here):
    rows_here = group_delta.shape[0]
    cols_here = group_delta.shape[1]
    pixels = rows_here * cols_here
    delta_groups = group_delta.reshape(pixels, groups_here, group_size)
    kernel_terms = []
    for row_shift in range(3):
        for col_shift in range(3):
            window = padded_first[
                row_shift : row_shift + rows_here, col_shift : col_shift + cols_here
            ]
            window = window.reshape(pixels, groups_here, group_size)
            kernel_terms.append(
                jnp.einsum("pgi,pgo->gio", window, delta_groups, preferred_element_type=jnp.float32)
            )
    kernel_part = jnp.stack(kernel_terms).reshape(3, 3, groups_here, group_size, group_size)
    kernel_part = jnp.transpose(kernel_part, (0, 1, 3, 2, 4))
    return kernel_part.reshape(3, 3, group_size, groups_here * group_size)


def body(images, first_weight, group_weight, third_weight, out_grad):
    rows_here = images.shape[0]
    cols_here = images.shape[1]
    group_size = group_weight.shape[2]
    first_panel, third_panel = (
        lax.all_gather(first_weight, "chan", axis=0, tiled=True),
        lax.all_gather(third_weight, "chan", axis=0, tiled=True),
    )
    pixels = rows_here * cols_here
    groups_here = group_weight.shape[3] // group_size
    gathered = lax.all_gather(images, "filt", axis=2, tiled=True)
    flat_images = gathered.reshape(pixels, gathered.shape[2])
    pre_first = jnp.dot(flat_images, first_panel, preferred_element_type=jnp.float32)
    act_first = (
        jax.nn.silu(pre_first)
        .astype(jnp.bfloat16)
        .reshape(rows_here, cols_here, first_panel.shape[1])
    )
    padded_first = extended(act_first, (("rows", 0), ("chan", 1)), 1)
    pre_group = group_conv(padded_first, group_weight, groups_here)
    act_group = jax.nn.silu(pre_group).astype(jnp.bfloat16)
    mid_whole = lax.all_gather(act_group, "filt", axis=2, tiled=True)
    flat_mid = mid_whole.reshape(pixels, mid_whole.shape[2])
    third_out = jnp.dot(flat_mid, third_panel, preferred_element_type=jnp.float32)
    own_images = images.reshape(pixels, images.shape[2]).astype(jnp.float32)
    block_out = (own_images + third_out).astype(jnp.bfloat16).reshape(images.shape)
    grad_flat = out_grad.reshape(pixels, out_grad.shape[2])
    mid_terms = lax.dot_general(
        grad_flat, third_panel, (((1,), (1,)), ((), ())), preferred_element_type=jnp.float32
    )
    mid_grad = lax.psum_scatter(
        mid_terms.reshape(rows_here, cols_here, mid_terms.shape[1]),
        "filt",
        scatter_dimension=2,
        tiled=True,
    )
    third_part = lax.dot_general(
        flat_mid, grad_flat, (((0,), (0,)), ((), ())), preferred_element_type=jnp.float32
    )
    group_delta = (mid_grad * silu_slope(pre_group)).astype(jnp.bfloat16)
    padded_delta = extended(group_delta, (("rows", 0), ("chan", 1)), 1)
    first_back = group_conv(
        padded_delta, transposed_kernel(group_weight, group_size, groups_here), groups_here
    )
    kernel_part = kernel_partial(padded_first, group_delta, group_size, groups_here)
    first_delta = (first_back.reshape(pixels, first_back.shape[2]) * silu_slope(pre_first)).astype(
        jnp.bfloat16
    )
    first_part = lax.dot_general(
        flat_images, first_delta, (((0,), (0,)), ((), ())), preferred_element_type=jnp.float32
    )
    input_terms = lax.dot_general(
        first_delta, first_panel, (((1,), (1,)), ((), ())), preferred_element_type=jnp.float32
    )
    back_images = lax.psum_scatter(
        input_terms.reshape(rows_here, cols_here, input_terms.shape[1]).astype(jnp.bfloat16),
        "filt",
        scatter_dimension=2,
        tiled=True,
    ).astype(jnp.float32)
    images_grad = out_grad.astype(jnp.float32) + back_images
    group_grad = lax.psum(kernel_part, ("rows", "chan"))
    first_total, third_total = lax.psum((first_part, third_part), "rows")
    first_grad, third_grad = (
        lax.psum_scatter(first_total, "chan", scatter_dimension=0, tiled=True),
        lax.psum_scatter(third_total, "chan", scatter_dimension=0, tiled=True),
    )
    return (block_out, images_grad, first_grad, group_grad, third_grad)


def solution(mesh):
    in_specs = (
        P("rows", "chan", "filt"),
        P("chan", "filt"),
        P(None, None, None, "filt"),
        P("chan", "filt"),
        P("rows", "chan", "filt"),
    )
    out_specs = (
        P("rows", "chan", "filt"),
        P("rows", "chan", "filt"),
        P("chan", "filt"),
        P(None, None, None, "filt"),
        P("chan", "filt"),
    )
    return jax.shard_map(body, mesh=mesh, in_specs=in_specs, out_specs=out_specs, check_vma=False)
```

profile of v0, /device:TPU:32, one launch (start us, length us, event | category | flops | bytes accessed | tf_op | source)
XLA Modules:
  0.0 700.0 jit_solution(2654013649618200023)
XLA Ops:
  7.9 39.6 %all_gather.15 = bf16[1024,256]{1,0:T(8,128)(2,1)S(1)} all-gather(bf16[128,256]{1,0:T(8,128)(2,1)} %param.8), channel_id=1, replica_groups=mesh['rows'=4,'chan'=8,'filt'=8] {'chan'}, dimensions={0}, use_global_device_ids=true | all-gather | bytes 589824 | tf_op jit(solution)/shard_map/all_gather | solution.py:72
  47.5 3.8 fusion.10
  52.2 36.9 %all_gather.13 = bf16[2048,128]{1,0:T(8,128)(2,1)S(1)} all-gather(bf16[256,128]{1,0:T(8,128)(2,1)S(1)} %copy-done.13), channel_id=1, replica_groups=mesh['rows'=4,'chan'=8,'filt'=8] {'chan'}, dimensions={0}, use_global_device_ids=true | all-gather | bytes 589824 | tf_op jit(solution)/shard_map/all_gather | solution.py:71
  89.1 4.4 multiply_convert_fusion.3
  93.5 2.9 collective-permute-start
  96.4 1.3 collective-permute-start.1
  98.4 4.2 collective-permute-done.1
  103.2 3.4 collective-permute-start.2
  106.6 3.2 collective-permute-start.3
  110.7 8.0 %collective-permute-done.2 = bf16[6,1,128]{1,2,0:T(8,128)(2,1)S(1)} collective-permute-done((bf16[6,1,128]{1,2,0:T(8,128)(2,1)S(1)}, bf16[6,1,128]{1,2,0:T(8,128)(2,1)S(1)}, u32[]{:S(2)}, u32[]{:S(2)}) %collective-permute-start.2) | collective-permute-done | bytes 1568 | tf_op jit(solution)/shard_map/ppermute | solution.py:12
  118.7 10.6 %collective-permute-done.3 = bf16[6,1,128]{1,2,0:T(8,128)(2,1)S(1)} collective-permute-done((bf16[6,1,128]{1,2,0:T(8,128)(2,1)S(1)}, bf16[6,1,128]{1,2,0:T(8,128)(2,1)S(1)}, u32[]{:S(2)}, u32[]{:S(2)}) %collective-permute-start.3) | collective-permute-done | bytes 1568 | tf_op jit(solution)/shard_map/ppermute | solution.py:15
  130.0 5.8 copy.36
  135.8 9.4 %fusion.13 = f32[1,4,256,4,32]{4,0,3,2,1:T(1,128)S(1)} fusion(bf16[1,6,258,4,32]{4,0,3,2,1:T(2,128)(2,1)} %copy.36, bf16[3,3,32,4,32]{4,3,2,1,0:T(4,128)(2,1)} %shard_map.94), kind=kOutput, calls=%fused_computation.39 | convolution fusion | flops 75497472 | bytes 994304 | tf_op jit(solution)/shard_map/conv_general_dilated | solution.py:26
  145.3 3.5 copy.38
  148.8 1.3 copy.40
  150.2 2.0 multiply_convert_fusion.1
  152.2 3.3 collective-permute-start.4
  155.6 1.3 collective-permute-start.5
  157.5 4.3 collective-permute-done.5
  161.8 3.5 collective-permute-start.6
  165.3 2.6 collective-permute-start.7
  169.2 2.5 collective-permute-done.7
  172.1 5.9 copy.44
  178.0 13.8 %convolution_reduce_fusion = f32[4,256,4,32]{3,2,1,0:T(4,128)S(1)} fusion(bf16[1,6,258,4,32]{4,0,3,2,1:T(2,128)(2,1)} %copy.44, bf16[3,3,32,4,32]{4,3,2,1,0:T(4,128)(2,1)} %rev.6), kind=kOutput, calls=%fused_computation.2 | convolution fusion | flops 75497472 | bytes 994304 | tf_op jit(solution)/shard_map/conv_general_dilated | solution.py:26
  191.8 1.7 reshape.99
  193.5 1.4 multiply_convert_fusion
  194.9 4.0 convolution_bitcast_fusion
  199.0 3.4 convolution_bitcast_fusion.1
  202.4 40.0 %reduce-scatter.9.cloned.1.call-done = f32[256,128]{0,1:T(8,128)} async-done(((f32[2048,128]{0,1:T(8,128)}), f32[256,128]{0,1:T(8,128)}) %reduce-scatter.9.cloned.1.call-update) | async-done | bytes 131088 | tf_op jit(solution)/shard_map/reduce_scatter | solution.py:130
  242.4 44.5 %reduce-scatter.11.cloned.1.call-done = f32[128,256]{1,0:T(8,128)} async-done(((f32[1024,256]{1,0:T(8,128)}), f32[128,256]{1,0:T(8,128)}) %reduce-scatter.11.cloned.1.call-update) | async-done | bytes 131088 | tf_op jit(solution)/shard_map/reduce_scatter | solution.py:131
  286.9 3.2 convolution_convert_fusion
  291.8 1.2 pad_maximum_fusion.1
  294.3 1.8 reshape.85
  297.0 1.1 reshape.88
  299.1 1.8 reshape.89
  302.2 1.1 reshape.91
  304.2 1.1 reshape.93
  306.2 1.1 reshape.86
  307.3 1.1 fusion.9
  308.9 1.2 fusion.6
  311.5 0.9 reshape.95
  312.5 3.2 fusion
  315.6 21.3 %all-reduce.6.cloned.1.call-done = (f32[256,128]{0,1:T(8,128)}, f32[128,256]{1,0:T(8,128)}) async-done(((f32[256,128]{0,1:T(8,128)}, f32[128,256]{1,0:T(8,128)}), (f32[256,128]{0,1:T(8,128)}, f32[128,256]{1,0:T(8,128)})) %all-reduce.6.cloned.1.call-update) | async-done | bytes 262160 | tf_op jit(solution)/shard_map/psum | solution.py:128
  337.0 1.7 copy.60
  338.7 59.3 %reduce-scatter.7.cloned.1.call-done = bf16[4,256,256]{2,1,0:T(8,128)(2,1)} async-done(((bf16[4,256,2048]{2,1,0:T(8,128)(2,1)}), bf16[4,256,256]{2,1,0:T(8,128)(2,1)}) %reduce-scatter.7.cloned.1.call-update) | async-done | bytes 524304 | tf_op jit(solution)/shard_map/reduce_scatter | solution.py:120
  398.0 2.1 convert_add_fusion
  400.1 290.7 %all-reduce.4.cloned.1.call-done = f32[3,3,32,128]{3,2,1,0:T(8,128)} async-done(((f32[3,3,32,128]{3,2,1,0:T(8,128)}), f32[3,3,32,128]{3,2,1,0:T(8,128)}) %all-reduce.4.cloned.1.call-update) | async-done | bytes 147472 | tf_op jit(solution)/shard_map/psum | solution.py:127
  690.9 1.6 copy.78
  (90 shorter events, 17.4 us)
Async XLA Ops:
  7.2 81.9 %all-gather.3.cloned.1.call-start = ((), (), s32[]{:S(2)}) async-start(), calls=%async_computation.4 | async-start | bytes 4718592 | tf_op jit(solution)/shard_map/all_gather | solution.py:76
  7.9 142.2 %reduce-scatter.5.cloned.1.call-start = ((), (), s32[]{:S(2)}) async-start(), calls=%async_computation.6 | async-start | bytes 4718592 | tf_op jit(solution)/shard_map/reduce_scatter | solution.py:96
  51.3 0.8 copy-start.13
  51.4 147.6 %all-gather.5.cloned.1.call-start = ((), (), s32[]{:S(2)}) async-start(), calls=%async_computation.5 | async-start | bytes 2359296 | tf_op jit(solution)/shard_map/all_gather | solution.py:87
  89.1 4.4 copy-start
  93.5 16.3 %copy-start.12 = (bf16[3,3,32,128]{3,2,1,0:T(8,128)(2,1)S(1)}, bf16[3,3,32,128]{3,2,1,0:T(8,128)(2,1)}, u32[]{:S(2)}) copy-start(bf16[3,3,32,128]{3,2,1,0:T(8,128)(2,1)} %param.7) | copy-start | bytes 221188
  93.5 4.8 collective-permute-start
  96.4 6.2 collective-permute-start.1
  98.3 4.6 copy-start.7
  102.6 0.6 copy-start.9
  103.2 15.5 %collective-permute-start.2 = (bf16[6,1,128]{1,2,0:T(8,128)(2,1)S(1)}, bf16[6,1,128]{1,2,0:T(8,128)(2,1)S(1)}, u32[]{:S(2)}, u32[]{:S(2)}) collective-permute-start(bf16[6,1,128]{1,2,0:T(8,128)(2,1)S(1)} %get-tuple-element.29), channel_id=1, source_target_pairs={{0,8},{8,16},{16,24},{24,32},{32,40},{40,48},{48,56},{1,9},{9,17},... | collective-permute-start | bytes 4616 | tf_op jit(solution)/shard_map/ppermute | solution.py:12
  106.6 22.7 %collective-permute-start.3 = (bf16[6,1,128]{1,2,0:T(8,128)(2,1)S(1)}, bf16[6,1,128]{1,2,0:T(8,128)(2,1)S(1)}, u32[]{:S(2)}, u32[]{:S(2)}) collective-permute-start(bf16[6,1,128]{1,2,0:T(8,128)(2,1)S(1)} %get-tuple-element.30), channel_id=1, source_target_pairs={{8,0},{16,8},{24,16},{32,24},{40,32},{48,40},{56,48},{9,1},{17,9},... | collective-permute-start | bytes 4616 | tf_op jit(solution)/shard_map/ppermute | solution.py:15
  118.7 17.1 %copy-start.4 = (bf16[6,1,128]{1,2,0:T(8,128)(2,1)}, bf16[6,1,128]{1,2,0:T(8,128)(2,1)S(1)}, u32[]{:S(2)}) copy-start(bf16[6,1,128]{1,2,0:T(8,128)(2,1)S(1)} %collective-permute-done.2) | copy-start | bytes 4612
  129.3 0.7 copy-start.6
  148.8 19.0 %copy-start.3 = (bf16[3,3,32,4,32]{4,3,2,1,0:T(4,128)(2,1)S(1)}, bf16[3,3,32,4,32]{4,3,2,1,0:T(4,128)(2,1)}, u32[]{:S(2)}) copy-start(bf16[3,3,32,4,32]{4,3,2,1,0:T(4,128)(2,1)} %shard_map.94) | copy-start | bytes 221188
  152.2 90.2 %reduce-scatter.9.cloned.1.call-start = ((), (), s32[]{:S(2)}) async-start(), calls=%async_computation.9 | async-start | bytes 1179648 | tf_op jit(solution)/shard_map/reduce_scatter | solution.py:130
  152.2 5.2 collective-permute-start.4
  155.6 6.2 collective-permute-start.5
  161.8 7.4 %collective-permute-start.6 = (bf16[6,1,128]{2,1,0:T(2,128)(2,1)S(1)}, bf16[6,1,128]{2,1,0:T(2,128)(2,1)S(1)}, u32[]{:S(2)}, u32[]{:S(2)}) collective-permute-start(bf16[6,1,128]{2,1,0:T(2,128)(2,1)S(1)} %get-tuple-element.27), channel_id=1, source_target_pairs={{0,8},{8,16},{16,24},{24,32},{32,40},{40,48},{48,56},{1,9},{9,17},... | collective-permute-start | bytes 4616 | tf_op jit(solution)/shard_map/ppermute | solution.py:12
  165.3 6.4 collective-permute-start.7
  194.9 4.1 copy-start.2
  198.9 88.0 %copy-start.1 = (bf16[2048,128]{1,0:T(8,128)(2,1)S(1)}, bf16[2048,128]{1,0:T(8,128)(2,1)}, u32[]{:S(2)}) copy-start(bf16[2048,128]{1,0:T(8,128)(2,1)} %copy-done) | copy-start | bytes 1572868
  198.9 88.0 %reduce-scatter.11.cloned.1.call-start = ((), (), s32[]{:S(2)}) async-start(), calls=%async_computation.10 | async-start | bytes 1179648 | tf_op jit(solution)/shard_map/reduce_scatter | solution.py:131
  202.4 134.6 %all-reduce.6.cloned.1.call-start = ((), (), s32[]{:S(2)}) async-start(), calls=%async_computation.11 | async-start | bytes 524288 | tf_op jit(solution)/shard_map/psum | solution.py:128
  286.9 111.1 %reduce-scatter.7.cloned.1.call-start = ((), (), s32[]{:S(2)}) async-start(), calls=%async_computation.7 | async-start | bytes 4718592 | tf_op jit(solution)/shard_map/reduce_scatter | solution.py:120
  290.2 0.8 copy-start.8
  290.2 0.9 copy-start.10
  290.2 1.6 copy-start.5
  290.2 400.7 %all-reduce.4.cloned.1.call-start = ((), (), s32[]{:S(2)}) async-start(), calls=%async_computation.8 | async-start | bytes 294912 | tf_op jit(solution)/shard_map/psum | solution.py:127
  337.0 355.5 %copy-start.11 = (f32[128,256]{1,0:T(8,128)S(1)}, f32[128,256]{1,0:T(8,128)}, u32[]{:S(2)}) copy-start(f32[128,256]{1,0:T(8,128)} %get-tuple-element.46) | copy-start | bytes 393220
Sparse Core Ops, SparseCore 0:
  9.8 60.3 all-gather.2
  72.7 76.7 reduce-scatter.4
  152.3 42.8 all-gather.4
  199.0 43.3 reduce-scatter.8
  244.8 42.0 reduce-scatter.10
  289.1 47.8 all-reduce.5
  339.7 58.2 reduce-scatter.6
  401.4 289.4 all-reduce.3
where the time goes:
time: 701 us; the launch traced here: 700 us
  waiting for transfers between devices  487 us (69%)
  blocking collectives  76.5 us (11%)
  matrix products  49 us (7%)
  local copies, waits for them, and re-layouts  43.4 us (6%)
  starting transfers between devices  22 us (3%)
  between operations  14.5 us (2%)
  other arithmetic  7.29 us (1%)
    psum x1, waiting for transfers between devices, body(): group_grad = lax.psum(kernel_part, ('rows', 'chan'))  291 us
    reduce_scatter x1, waiting for transfers between devices, body(): lax.psum_scatter(input_terms.reshape(rows_here, cols_here, input_terms.sh...  59.3 us
    reduce_scatter x1, waiting for transfers between devices, body(): lax.psum_scatter(third_total, 'chan', scatter_dimension=0, tiled=True)  44.5 us
    reduce_scatter x1, waiting for transfers between devices, body(): lax.psum_scatter(first_total, 'chan', scatter_dimension=0, tiled=True)  40 us
    all_gather x1, blocking collectives, body(): lax.all_gather(third_weight, 'chan', axis=0, tiled=True)  39.6 us
    all_gather x1, blocking collectives, body(): lax.all_gather(first_weight, 'chan', axis=0, tiled=True)  36.9 us
    conv_general_dilated x2, matrix products, group_conv(): lax.conv_general_dilated(padded[None], kernel, (1, 1), 'VALID', dimension...  23.3 us
    ppermute x4, waiting for transfers between devices, extended(): lax.ppermute(lax.slice_in_dim(block, 0, width, axis=dim), axis, backward)  21.5 us
  transfers between devices with their start and end apart: 16, of which 12 were waited for; matrix products, arithmetic and copies ran while one was open for 13% of the time, Pallas kernels for 0%

commit v1 on v0

--- a/solution.py
+++ b/solution.py
@@ -68,7 +68,9 @@
     cols_here = images.shape[1]
     group_size = group_weight.shape[2]
     first_panel, third_panel = (
-        lax.all_gather(first_weight, "chan", axis=0, tiled=True),
+        jnp.concatenate(
+            lax.all_to_all(jnp.stack([first_weight] * lax.axis_size("chan")), "chan", 0, 0), axis=0
+        ),
         lax.all_gather(third_weight, "chan", axis=0, tiled=True),
     )
     pixels = rows_here * cols_here

time: 701 us -> 693 us (0.989)
  blocking collectives: 76.5 us -> 56.7 us
  starting transfers between devices: 22 us -> 29.1 us
    all_gather x1 -> x0, blocking collectives: 36.9 us -> none  [body(): lax.all_gather(first_weight, 'chan', axis=0, tiled=True)]
    all_to_all x0 -> x1, blocking collectives: none -> 17.3 us  [body(): lax.all_to_all(jnp.stack([first_weight] * lax.axis_size('chan')), 'chan',...]
  transfers between devices with their start and end apart: 16 -> 16, of which waited for: 12 -> 14; matrix products, arithmetic and copies ran while one was open for 13% -> 14% of each run, Pallas kernels for 0% -> 0%
where the time goes in v1:
time: 693 us; the launch traced here: 692 us
  waiting for transfers between devices  492 us (71%)
  blocking collectives  56.7 us (8%)
  matrix products  48.8 us (7%)
  local copies, waits for them, and re-layouts  43.5 us (6%)
  starting transfers between devices  29.1 us (4%)
  between operations  14.5 us (2%)
  other arithmetic  7.27 us (1%)
    psum x1, waiting for transfers between devices, body(): group_grad = lax.psum(kernel_part, ('rows', 'chan'))  291 us
    reduce_scatter x1, waiting for transfers between devices, body(): lax.psum_scatter(input_terms.reshape(rows_here, cols_here, input_terms.sh...  59.3 us
    reduce_scatter x1, waiting for transfers between devices, body(): lax.psum_scatter(third_total, 'chan', scatter_dimension=0, tiled=True)  44.4 us
    all_gather x1, blocking collectives, body(): lax.all_gather(third_weight, 'chan', axis=0, tiled=True)  39.4 us
    reduce_scatter x1, waiting for transfers between devices, body(): lax.psum_scatter(first_total, 'chan', scatter_dimension=0, tiled=True)  37.8 us
    ppermute x4, waiting for transfers between devices, extended(): lax.ppermute(lax.slice_in_dim(block, 0, width, axis=dim), axis, backward)  25.3 us
    conv_general_dilated x2, matrix products, group_conv(): lax.conv_general_dilated(padded[None], kernel, (1, 1), 'VALID', dimension...  23.3 us
    psum x1, waiting for transfers between devices, body(): first_total, third_total = lax.psum((first_part, third_part), 'rows')  21.3 us
  transfers between devices with their start and end apart: 16, of which 14 were waited for; matrix products, arithmetic and copies ran while one was open for 14% of the time, Pallas kernels for 0%

profile of v1, /device:TPU:32, one launch (start us, length us, event | category | flops | bytes accessed | tf_op | source)
XLA Modules:
  0.0 692.4 jit_solution(12058445084392213239)
XLA Ops:
  7.9 39.4 %all_gather.11 = bf16[1024,256]{1,0:T(8,128)(2,1)S(1)} all-gather(bf16[128,256]{1,0:T(8,128)(2,1)} %param.8), channel_id=1, replica_groups=mesh['rows'=4,'chan'=8,'filt'=8] {'chan'}, dimensions={0}, use_global_device_ids=true | all-gather | bytes 589824 | tf_op jit(solution)/shard_map/all_gather | solution.py:74
  47.4 3.8 fusion.10
  52.1 17.3 %all_to_all.5 = bf16[8,256,128]{2,1,0:T(8,128)(2,1)S(1)} all-to-all(bf16[8,256,128]{2,1,0:T(8,128)(2,1)S(1)} %stack.41), channel_id=1, replica_groups=mesh['rows'=4,'chan'=8,'filt'=8] {'chan'}, dimensions={0} | all-to-all | bytes 1048576 | tf_op jit(solution)/shard_map/all_to_all | solution.py:72
  69.7 4.2 multiply_convert_fusion.3
  73.9 4.2 collective-permute-start
  78.2 1.3 collective-permute-start.1
  80.2 4.2 collective-permute-done.1
  84.9 10.2 %collective-permute-start.2 = (bf16[6,1,128]{1,2,0:T(8,128)(2,1)S(1)}, bf16[6,1,128]{1,2,0:T(8,128)(2,1)S(1)}, u32[]{:S(2)}, u32[]{:S(2)}) collective-permute-start(bf16[6,1,128]{1,2,0:T(8,128)(2,1)S(1)} %get-tuple-element.29), channel_id=1, source_target_pairs={{0,8},{8,16},{16,24},{24,32},{32,40},{40,48},{48,56},{1,9},{9,17},... | collective-permute-start | bytes 4616 | tf_op jit(solution)/shard_map/ppermute | solution.py:12
  95.1 2.1 collective-permute-start.3
  98.1 7.9 %collective-permute-done.2 = bf16[6,1,128]{1,2,0:T(8,128)(2,1)S(1)} collective-permute-done((bf16[6,1,128]{1,2,0:T(8,128)(2,1)S(1)}, bf16[6,1,128]{1,2,0:T(8,128)(2,1)S(1)}, u32[]{:S(2)}, u32[]{:S(2)}) %collective-permute-start.2) | collective-permute-done | bytes 1568 | tf_op jit(solution)/shard_map/ppermute | solution.py:12
  106.1 15.8 %collective-permute-done.3 = bf16[6,1,128]{1,2,0:T(8,128)(2,1)S(1)} collective-permute-done((bf16[6,1,128]{1,2,0:T(8,128)(2,1)S(1)}, bf16[6,1,128]{1,2,0:T(8,128)(2,1)S(1)}, u32[]{:S(2)}, u32[]{:S(2)}) %collective-permute-start.3) | collective-permute-done | bytes 1568 | tf_op jit(solution)/shard_map/ppermute | solution.py:15
  122.6 5.8 copy.36
  128.4 9.5 %fusion.13 = f32[1,4,256,4,32]{4,0,3,2,1:T(1,128)S(1)} fusion(bf16[1,6,258,4,32]{4,0,3,2,1:T(2,128)(2,1)} %copy.36, bf16[3,3,32,4,32]{4,3,2,1,0:T(4,128)(2,1)} %shard_map.94), kind=kOutput, calls=%fused_computation.39 | convolution fusion | flops 75497472 | bytes 994304 | tf_op jit(solution)/shard_map/conv_general_dilated | solution.py:26
  137.9 3.5 copy.38
  141.4 1.3 copy.40
  142.7 3.5 reduce-scatter.5.cloned.1.call-done
  146.2 2.0 multiply_convert_fusion.1
  148.3 3.4 collective-permute-start.4
  151.7 1.3 collective-permute-start.5
  153.6 4.3 collective-permute-done.5
  157.9 2.1 collective-permute-start.6
  160.0 4.0 collective-permute-start.7
  165.3 1.1 collective-permute-done.7
  166.8 5.9 copy.44
  172.7 13.8 %convolution_reduce_fusion = f32[4,256,4,32]{3,2,1,0:T(4,128)S(1)} fusion(bf16[1,6,258,4,32]{4,0,3,2,1:T(2,128)(2,1)} %copy.44, bf16[3,3,32,4,32]{4,3,2,1,0:T(4,128)(2,1)} %rev.6), kind=kOutput, calls=%fused_computation.2 | convolution fusion | flops 75497472 | bytes 994304 | tf_op jit(solution)/shard_map/conv_general_dilated | solution.py:26
  186.5 1.7 reshape.106
  188.2 1.4 multiply_convert_fusion
  189.6 4.0 convolution_bitcast_fusion
  193.7 3.4 convolution_bitcast_fusion.1
  197.1 37.8 %reduce-scatter.9.cloned.1.call-done = f32[256,128]{0,1:T(8,128)} async-done(((f32[2048,128]{0,1:T(8,128)}), f32[256,128]{0,1:T(8,128)}) %reduce-scatter.9.cloned.1.call-update) | async-done | bytes 131088 | tf_op jit(solution)/shard_map/reduce_scatter | solution.py:132
  234.9 44.4 %reduce-scatter.11.cloned.1.call-done = f32[128,256]{1,0:T(8,128)} async-done(((f32[1024,256]{1,0:T(8,128)}), f32[128,256]{1,0:T(8,128)}) %reduce-scatter.11.cloned.1.call-update) | async-done | bytes 131088 | tf_op jit(solution)/shard_map/reduce_scatter | solution.py:133
  279.4 3.2 convolution_convert_fusion
  284.2 1.2 pad_maximum_fusion.1
  286.7 1.8 reshape.91
  289.4 1.1 reshape.94
  291.5 1.8 reshape.95
  294.6 1.1 reshape.97
  296.6 1.1 reshape.99
  298.6 1.1 reshape.92
  299.7 1.1 fusion.9
  301.3 1.2 fusion.6
  304.9 3.2 fusion
  308.1 21.3 %all-reduce.6.cloned.1.call-done = (f32[256,128]{0,1:T(8,128)}, f32[128,256]{1,0:T(8,128)}) async-done(((f32[256,128]{0,1:T(8,128)}, f32[128,256]{1,0:T(8,128)}), (f32[256,128]{0,1:T(8,128)}, f32[128,256]{1,0:T(8,128)})) %all-reduce.6.cloned.1.call-update) | async-done | bytes 262160 | tf_op jit(solution)/shard_map/psum | solution.py:130
  329.4 1.7 copy.60
  331.1 59.3 %reduce-scatter.7.cloned.1.call-done = bf16[4,256,256]{2,1,0:T(8,128)(2,1)} async-done(((bf16[4,256,2048]{2,1,0:T(8,128)(2,1)}), bf16[4,256,256]{2,1,0:T(8,128)(2,1)}) %reduce-scatter.7.cloned.1.call-update) | async-done | bytes 524304 | tf_op jit(solution)/shard_map/reduce_scatter | solution.py:122
  390.4 2.1 convert_add_fusion
  392.5 290.7 %all-reduce.4.cloned.1.call-done = f32[3,3,32,128]{3,2,1,0:T(8,128)} async-done(((f32[3,3,32,128]{3,2,1,0:T(8,128)}), f32[3,3,32,128]{3,2,1,0:T(8,128)}) %all-reduce.4.cloned.1.call-update) | async-done | bytes 147472 | tf_op jit(solution)/shard_map/psum | solution.py:129
  683.3 1.6 copy.78
  (91 shorter events, 18.7 us)
Async XLA Ops:
  7.2 62.5 %all-gather.3.cloned.1.call-start = ((), (), s32[]{:S(2)}) async-start(), calls=%async_computation.5 | async-start | bytes 4718592 | tf_op jit(solution)/shard_map/all_gather | solution.py:78
  7.9 138.3 %reduce-scatter.5.cloned.1.call-start = ((), (), s32[]{:S(2)}) async-start(), calls=%async_computation.7 | async-start | bytes 4718592 | tf_op jit(solution)/shard_map/reduce_scatter | solution.py:98
  51.2 0.8 copy-start.13
  51.2 142.5 %all-gather.5.cloned.1.call-start = ((), (), s32[]{:S(2)}) async-start(), calls=%async_computation.6 | async-start | bytes 2359296 | tf_op jit(solution)/shard_map/all_gather | solution.py:89
  69.4 4.5 copy-start
  73.9 23.3 %copy-start.12 = (bf16[3,3,32,128]{3,2,1,0:T(8,128)(2,1)S(1)}, bf16[3,3,32,128]{3,2,1,0:T(8,128)(2,1)}, u32[]{:S(2)}) copy-start(bf16[3,3,32,128]{3,2,1,0:T(8,128)(2,1)} %param.7) | copy-start | bytes 221188
  73.9 6.1 collective-permute-start
  78.2 6.2 collective-permute-start.1
  80.0 4.6 copy-start.7
  84.3 0.6 copy-start.9
  84.9 21.1 %collective-permute-start.2 = (bf16[6,1,128]{1,2,0:T(8,128)(2,1)S(1)}, bf16[6,1,128]{1,2,0:T(8,128)(2,1)S(1)}, u32[]{:S(2)}, u32[]{:S(2)}) collective-permute-start(bf16[6,1,128]{1,2,0:T(8,128)(2,1)S(1)} %get-tuple-element.29), channel_id=1, source_target_pairs={{0,8},{8,16},{16,24},{24,32},{32,40},{40,48},{48,56},{1,9},{9,17},... | collective-permute-start | bytes 4616 | tf_op jit(solution)/shard_map/ppermute | solution.py:12
  95.1 26.8 %collective-permute-start.3 = (bf16[6,1,128]{1,2,0:T(8,128)(2,1)S(1)}, bf16[6,1,128]{1,2,0:T(8,128)(2,1)S(1)}, u32[]{:S(2)}, u32[]{:S(2)}) collective-permute-start(bf16[6,1,128]{1,2,0:T(8,128)(2,1)S(1)} %get-tuple-element.30), channel_id=1, source_target_pairs={{8,0},{16,8},{24,16},{32,24},{40,32},{48,40},{56,48},{9,1},{17,9},... | collective-permute-start | bytes 4616 | tf_op jit(solution)/shard_map/ppermute | solution.py:15
  106.1 22.4 %copy-start.4 = (bf16[6,1,128]{1,2,0:T(8,128)(2,1)}, bf16[6,1,128]{1,2,0:T(8,128)(2,1)S(1)}, u32[]{:S(2)}) copy-start(bf16[6,1,128]{1,2,0:T(8,128)(2,1)S(1)} %collective-permute-done.2) | copy-start | bytes 4612
  121.9 0.7 copy-start.6
  141.4 22.6 %copy-start.3 = (bf16[3,3,32,4,32]{4,3,2,1,0:T(4,128)(2,1)S(1)}, bf16[3,3,32,4,32]{4,3,2,1,0:T(4,128)(2,1)}, u32[]{:S(2)}) copy-start(bf16[3,3,32,4,32]{4,3,2,1,0:T(4,128)(2,1)} %shard_map.94) | copy-start | bytes 221188
  148.2 86.7 %reduce-scatter.9.cloned.1.call-start = ((), (), s32[]{:S(2)}) async-start(), calls=%async_computation.10 | async-start | bytes 1179648 | tf_op jit(solution)/shard_map/reduce_scatter | solution.py:132
  148.3 5.3 collective-permute-start.4
  151.7 6.2 collective-permute-start.5
  157.9 7.4 %collective-permute-start.6 = (bf16[6,1,128]{2,1,0:T(2,128)(2,1)S(1)}, bf16[6,1,128]{2,1,0:T(2,128)(2,1)S(1)}, u32[]{:S(2)}, u32[]{:S(2)}) collective-permute-start(bf16[6,1,128]{2,1,0:T(2,128)(2,1)S(1)} %get-tuple-element.27), channel_id=1, source_target_pairs={{0,8},{8,16},{16,24},{24,32},{32,40},{40,48},{48,56},{1,9},{9,17},... | collective-permute-start | bytes 4616 | tf_op jit(solution)/shard_map/ppermute | solution.py:12
  160.0 6.4 collective-permute-start.7
  189.6 4.1 copy-start.2
  193.6 85.7 %copy-start.1 = (bf16[8,256,128]{2,1,0:T(8,128)(2,1)S(1)}, bf16[8,256,128]{2,1,0:T(8,128)(2,1)}, u32[]{:S(2)}) copy-start(bf16[8,256,128]{2,1,0:T(8,128)(2,1)} %copy-done) | copy-start | bytes 1572868
  193.6 85.7 %reduce-scatter.11.cloned.1.call-start = ((), (), s32[]{:S(2)}) async-start(), calls=%async_computation.11 | async-start | bytes 1179648 | tf_op jit(solution)/shard_map/reduce_scatter | solution.py:133
  197.1 132.3 %all-reduce.6.cloned.1.call-start = ((), (), s32[]{:S(2)}) async-start(), calls=%async_computation.12 | async-start | bytes 524288 | tf_op jit(solution)/shard_map/psum | solution.py:130
  279.3 111.1 %reduce-scatter.7.cloned.1.call-start = ((), (), s32[]{:S(2)}) async-start(), calls=%async_computation.8 | async-start | bytes 4718592 | tf_op jit(solution)/shard_map/reduce_scatter | solution.py:122
  282.6 0.8 copy-start.8
  282.6 0.9 copy-start.10
  282.6 1.6 copy-start.5
  282.6 400.7 %all-reduce.4.cloned.1.call-start = ((), (), s32[]{:S(2)}) async-start(), calls=%async_computation.9 | async-start | bytes 294912 | tf_op jit(solution)/shard_map/psum | solution.py:129
  329.4 355.5 %copy-start.11 = (f32[128,256]{1,0:T(8,128)S(1)}, f32[128,256]{1,0:T(8,128)}, u32[]{:S(2)}) copy-start(f32[128,256]{1,0:T(8,128)} %get-tuple-element.46) | copy-start | bytes 393220
Sparse Core Ops, SparseCore 0:
  9.8 59.8 all-gather.2
  72.3 73.8 reduce-scatter.4
  148.3 36.9 all-gather.4
  193.7 41.1 reduce-scatter.8
  237.3 41.9 reduce-scatter.10
  281.5 47.8 all-reduce.5
  332.1 58.2 reduce-scatter.6
  393.8 289.4 all-reduce.3
